TPU v7x, 512 devices: a whole 4x8x8 slice. The times are simulated.
512 devices in a mesh: ctx: 64 (over x, z, core), grp: 8 (over y).
Axes of the slice: x: 4, y: 8, z: 8, core: 2. Of those that a mesh axis runs over, the one named last changes fastest.
Arguments:
- queries: bfloat16 [131072, 2560], P(('ctx', 'grp')), may hold values from -40 to 40
- key_value_rows: bfloat16 [131072, 1024], P(('ctx', 'grp')), may hold values from -20 to 20
- unit_slot: int32 [256], replicated, may hold values from 0 to 255, as said below
- unit_doc: int32 [256], replicated, may hold values from 0 to 127, as said below
Outputs:
- attended: bfloat16 [131072, 2560], P(('ctx', 'grp'))
Inputs may be any that keep to these rules, and one draw needn't show every extreme that they name: `unit_slot`: A permutation of the slots; the units of one document, in stream order, take consecutive slots of one aligned block of 4 slots, and each block is filled by whole documents. `unit_doc`: starts at 0 and rises by one where a new document begins; a document holds 1 to 4 units.
All inputs are finite; a program needn't handle non-finite values.
Results may differ from a plain program's by a relative error of at most 0.007.
Values may be sent and summed in bfloat16 or wider, within the bound.
A program may use at most 64 MiB of HBM per device.

v0:
```python
import math

import jax
import jax.numpy as jnp
from jax import lax
from jax.sharding import PartitionSpec as P

QUERY_HEADS = 20
KEY_VALUE_HEADS = 4
HEAD_SIZE = 128


minimum_score = -1e30


def local(queries, key_value_rows, unit_slot, unit_doc):
    count_of_rows = queries.shape[0]
    ctx_count = lax.axis_size("ctx")
    grp_count = lax.axis_size("grp")
    unit_count = count_of_rows // ctx_count
    shards = ctx_count * grp_count
    query_per_key_heads = QUERY_HEADS // KEY_VALUE_HEADS
    inverse_root = 1.0 / math.sqrt(HEAD_SIZE)
    slot_unit = jnp.argsort(unit_slot)
    outgoing = (jnp.take(queries, slot_unit, axis=0), jnp.take(key_value_rows, slot_unit, axis=0))
    device_query, local_pairs = (
        lax.all_to_all(outgoing[0], "ctx", split_axis=0, concat_axis=0, tiled=True),
        lax.all_to_all(outgoing[1], "ctx", split_axis=0, concat_axis=0, tiled=True),
    )
    group_units = lax.dynamic_slice_in_dim(
        slot_unit, lax.axis_index("ctx") * unit_count, unit_count
    )
    row_unit = jnp.tile(group_units, ctx_count)
    row_source = jnp.arange(count_of_rows, dtype=jnp.int32) // unit_count
    base_position = row_unit * shards + row_source * grp_count
    row_document = jnp.take(unit_doc, row_unit)
    query_position = base_position + lax.axis_index("grp")
    head_grouped = device_query.reshape(
        count_of_rows, KEY_VALUE_HEADS, query_per_key_heads, HEAD_SIZE
    )
    initial = (
        jnp.full((KEY_VALUE_HEADS, query_per_key_heads, count_of_rows), minimum_score, jnp.float32),
        jnp.zeros((KEY_VALUE_HEADS, query_per_key_heads, count_of_rows), jnp.float32),
        jnp.zeros((count_of_rows, KEY_VALUE_HEADS, query_per_key_heads, HEAD_SIZE), jnp.float32),
    )
    gathered = lax.all_gather(local_pairs, "grp", axis=0, tiled=True)
    key_count = gathered.shape[0]

    def one_block(block_turn, state):
        running_max, running_sum, weighted = state
        offset = block_turn * count_of_rows
        rows_per_block = lax.dynamic_slice_in_dim(gathered, offset, count_of_rows, 0)
        key_head_rows = rows_per_block[:, : KEY_VALUE_HEADS * HEAD_SIZE].reshape(
            count_of_rows, KEY_VALUE_HEADS, HEAD_SIZE
        )
        value_head_rows = rows_per_block[:, KEY_VALUE_HEADS * HEAD_SIZE :].reshape(
            count_of_rows, KEY_VALUE_HEADS, HEAD_SIZE
        )
        where_ids = 0 + offset + jnp.arange(count_of_rows, dtype=jnp.int32)
        local_rows = where_ids % count_of_rows
        key_position = jnp.take(base_position, local_rows) + where_ids // count_of_rows
        key_document = jnp.take(row_document, local_rows)
        allowed = (key_document[None, :] == row_document[:, None]) & (
            key_position[None, :] <= query_position[:, None]
        )
        scores = (
            jnp.einsum(
                "qhgd,khd->hgqk", head_grouped, key_head_rows, preferred_element_type=jnp.float32
            )
            * inverse_root
        )
        masked = jnp.where(allowed, scores, minimum_score)
        newest_max = jnp.maximum(running_max, jnp.max(masked, axis=-1))
        exponent = jnp.where(allowed, jnp.exp(scores - newest_max[..., None]), 0.0)
        factor = jnp.exp(running_max - newest_max)
        running_sum = running_sum * factor + jnp.sum(exponent, axis=-1)
        weights = exponent.astype(jnp.bfloat16)
        update = jnp.einsum(
            "hgqk,khd->qhgd", weights, value_head_rows, preferred_element_type=jnp.float32
        )
        weighted = weighted * jnp.transpose(factor, (2, 0, 1))[..., None] + update
        return (newest_max, running_sum, weighted)

    running_max, running_sum, weighted = lax.fori_loop(
        0, key_count // count_of_rows, one_block, initial
    )
    result = weighted / jnp.transpose(running_sum, (2, 0, 1))[..., None]
    return result.reshape(count_of_rows, QUERY_HEADS * HEAD_SIZE).astype(jnp.bfloat16)


def solution(mesh):
    in_specs = (P(("ctx", "grp"), None), P(("ctx", "grp"), None), P(), P())
    out_specs = P(("ctx", "grp"), None)
    return jax.shard_map(local, mesh=mesh, in_specs=in_specs, out_specs=out_specs, check_vma=False)
```

profile of v0, /device:TPU:1, one launch (start us, length us, event | category | flops | bytes accessed | tf_op | source)
XLA Modules:
  0.0 260.8 jit_solution(10569352272624481808)
XLA Ops:
  6.5 3.9 %sort.17 = (s32[256]{0:T(256)}, s32[256]{0:T(256)S(1)}) sort(s32[256]{0:T(256)} %param.10, s32[256]{0:T(256)S(1)} %iota.17), dimensions={0}, to_apply=%region_0.0 | sort | flops 2048 | bytes 4096 | tf_op jit(solution)/shard_map/jit(argsort)/sort | solution.py:24
  10.6 2.7 %gather_fusion.2 = bf16[256,1024]{1,0:T(8,128)(2,1)S(1)} fusion(bf16[256,1024]{1,0:T(8,128)(2,1)} %param.9, s32[1024]{0:T(1024)S(1)} %pad_clamp_fusion.1), kind=kCustom, calls=%fused_computation.3 | custom fusion | bytes 1049600 | tf_op jit(solution)/shard_map/jit(_take)/gather | solution.py:25
  13.8 32.0 %all_to_all.15 = bf16[64,4,1024]{2,1,0:T(4,128)(2,1)S(1)} all-to-all(bf16[64,4,1024]{2,1,0:T(4,128)(2,1)S(1)} %broadcast_select_fusion.2), channel_id=1, replica_groups=mesh['ctx'=64,'grp'=8] {'ctx'}, dimensions={0} | all-to-all | bytes 1048576 | tf_op jit(solution)/shard_map/all_to_all | solution.py:28
  49.4 3.1 %broadcast_select_fusion.1 = bf16[64,4,2560]{2,1,0:T(4,128)(2,1)} fusion(bf16[64,4,2560]{2,1,0:T(4,128)(2,1)} %gather.18, pred[64,4]{1,0:T(8,128)(4,1)S(1)} %broadcast_in_dim.94), kind=kLoop, calls=%fused_computation.51 | loop fusion | flops 655360 | bytes 2621696 | tf_op jit(solution)/shard_map/jit(_take)/select_n | solution.py:25
  52.5 6.3 %all-to-all-start.1 = ((bf16[64,4,2560]{2,1,0:T(4,128)(2,1)}), bf16[64,4,2560]{2,1,0:T(4,128)(2,1)S(1)}, u32[]{:S(2)}, u32[]{:S(2)}) async-start(bf16[64,4,2560]{2,1,0:T(4,128)(2,1)} %broadcast_select_fusion.1), calls=%async_computation.1 | async-start | bytes 2621440 | tf_op jit(solution)/shard_map/all_to_all | solution.py:27
  59.1 1.9 gather_fusion.4
  61.0 31.9 %all-to-all-done.1 = bf16[64,4,2560]{2,1,0:T(4,128)(2,1)S(1)} async-done(((bf16[64,4,2560]{2,1,0:T(4,128)(2,1)}), bf16[64,4,2560]{2,1,0:T(4,128)(2,1)S(1)}, u32[]{:S(2)}, u32[]{:S(2)}) %all-to-all-start.1) | async-done | bytes 1310752 | tf_op jit(solution)/shard_map/all_to_all | solution.py:27
  93.0 2.4 reshape.59
  95.4 2.2 copy.11
  97.6 3.4 %all-gather.2.cloned.1.call-done = bf16[2048,1024]{1,0:T(8,128)(2,1)} async-done(((bf16[256,1024]{1,0:T(8,128)(2,1)}), bf16[2048,1024]{1,0:T(8,128)(2,1)}) %all-gather.2.cloned.1.call-update) | async-done | bytes 4194320 | tf_op jit(solution)/shard_map/all_gather | solution.py:46
  101.0 149.3 %while.22 = (s32[]{:T(128)}, f32[4,5,256]{2,1,0:T(8,128)S(1)}, f32[4,5,256]{2,1,0:T(8,128)S(1)}, f32[256,4,5,128]{0,3,2,1:T(8,128)}, s32[256]{0:T(256)S(1)}, /*i...) while((s32[]{:T(128)}, f32[4,5,256]{2,1,0:T(8,128)S(1)}, ...), condition=%wide.region_4.6_spmd.clone.clone.clone, body=%wide.region_1.5_spmd.clone.clone.clone.sunk | while | flops 687715328 | bytes 25520368 | solution.py:84
  101.1 1.9 gather_fusion
  103.1 1.9 gather_fusion.1
  106.4 3.4 %fusion.46 = (f32[4,5,256]{2,1,0:T(8,128)S(1)}, f32[4,256,256,5]{2,1,3,0:T(8,128)}) fusion(pred[256,256]{0,1:T(8,128)(4,1)S(1)} %compare_and_fusion.4, bf16[256,4,128,1]{0,2,3,1:T(8,128)(2,1)S(1)} %bitcast.56, bf16[256,4,5,128]{3,0,2,1:T(8,128)(2,1)S(1)} %get-tuple-element.467), kind=kOutput, calls=%fused_computation.9.clone.1 | convolution fusion | flops 339471360 | bytes 6901760 | tf_op jit(solution)/shard_map/while/body/eval_jaxpr/qhgd,khd->hgqk/dot_general | solution.py:67
  109.9 5.3 %bitcast_add_fusion.2 = f32[256,4,5,128]{0,3,2,1:T(8,128)} fusion(f32[256,4,5,128]{0,3,2,1:T(8,128)} %get-tuple-element.450, f32[256,4,5]{0,2,1:T(8,128)S(1)} %get-tuple-element.431, pred[]{:T(512)S(6)} %compare.22, bf16[256,4,128,1]{0,2,3,1:T(8,128)(2,1)S(1)} %bitcast.55, f32[4,256,256,5]{2,1,3,0:T(8,128)} %get-tuple-element.430, ...), kind=kOutput, calls=%fused_computation.15.clone.1 | convolution fusion | flops 342753280 | bytes 10854401 | tf_op jit(solution)/shard_map/while/body/eval_jaxpr/hgqk,khd->qhgd/dot_general | solution.py:78
  115.3 3.6 %fusion.48 = f32[4,5,256]{2,1,0:T(8,128)S(1)} fusion(f32[4,256,256,5]{2,1,3,0:T(8,128)} %get-tuple-element.430, f32[4,5,256]{2,1,0:T(8,128)S(1)} %get-tuple-element.462, pred[256,256]{0,1:T(8,128)(4,1)S(1)} %compare_and_fusion.4), kind=kLoop, calls=%fused_computation.13.clone.1 | loop fusion | flops 5237760 | bytes 5349376 | tf_op jit(solution)/shard_map/while/body/eval_jaxpr/reduce_sum | solution.py:76
  119.1 1.9 gather_fusion
  121.0 1.9 gather_fusion.1
  124.4 3.4 %fusion.46 = (f32[4,5,256]{2,1,0:T(8,128)S(1)}, f32[4,256,256,5]{2,1,3,0:T(8,128)}) fusion(pred[256,256]{0,1:T(8,128)(4,1)S(1)} %compare_and_fusion.4, bf16[256,4,128,1]{0,2,3,1:T(8,128)(2,1)S(1)} %bitcast.56, bf16[256,4,5,128]{3,0,2,1:T(8,128)(2,1)S(1)} %get-tuple-element.467), kind=kOutput, calls=%fused_computation.9.clone.1 | convolution fusion | flops 339471360 | bytes 6901760 | tf_op jit(solution)/shard_map/while/body/eval_jaxpr/qhgd,khd->hgqk/dot_general | solution.py:67
  127.9 6.2 %bitcast_add_fusion.2 = f32[256,4,5,128]{0,3,2,1:T(8,128)} fusion(f32[256,4,5,128]{0,3,2,1:T(8,128)} %get-tuple-element.450, f32[256,4,5]{0,2,1:T(8,128)S(1)} %get-tuple-element.431, pred[]{:T(512)S(6)} %compare.22, bf16[256,4,128,1]{0,2,3,1:T(8,128)(2,1)S(1)} %bitcast.55, f32[4,256,256,5]{2,1,3,0:T(8,128)} %get-tuple-element.430, ...), kind=kOutput, calls=%fused_computation.15.clone.1 | convolution fusion | flops 342753280 | bytes 10854401 | tf_op jit(solution)/shard_map/while/body/eval_jaxpr/hgqk,khd->qhgd/dot_general | solution.py:78
  134.1 3.6 %fusion.48 = f32[4,5,256]{2,1,0:T(8,128)S(1)} fusion(f32[4,256,256,5]{2,1,3,0:T(8,128)} %get-tuple-element.430, f32[4,5,256]{2,1,0:T(8,128)S(1)} %get-tuple-element.462, pred[256,256]{0,1:T(8,128)(4,1)S(1)} %compare_and_fusion.4), kind=kLoop, calls=%fused_computation.13.clone.1 | loop fusion | flops 5237760 | bytes 5349376 | tf_op jit(solution)/shard_map/while/body/eval_jaxpr/reduce_sum | solution.py:76
  137.8 1.9 gather_fusion
  139.8 1.9 gather_fusion.1
  143.1 3.4 %fusion.46 = (f32[4,5,256]{2,1,0:T(8,128)S(1)}, f32[4,256,256,5]{2,1,3,0:T(8,128)}) fusion(pred[256,256]{0,1:T(8,128)(4,1)S(1)} %compare_and_fusion.4, bf16[256,4,128,1]{0,2,3,1:T(8,128)(2,1)S(1)} %bitcast.56, bf16[256,4,5,128]{3,0,2,1:T(8,128)(2,1)S(1)} %get-tuple-element.467), kind=kOutput, calls=%fused_computation.9.clone.1 | convolution fusion | flops 339471360 | bytes 6901760 | tf_op jit(solution)/shard_map/while/body/eval_jaxpr/qhgd,khd->hgqk/dot_general | solution.py:67
  146.6 6.2 %bitcast_add_fusion.2 = f32[256,4,5,128]{0,3,2,1:T(8,128)} fusion(f32[256,4,5,128]{0,3,2,1:T(8,128)} %get-tuple-element.450, f32[256,4,5]{0,2,1:T(8,128)S(1)} %get-tuple-element.431, pred[]{:T(512)S(6)} %compare.22, bf16[256,4,128,1]{0,2,3,1:T(8,128)(2,1)S(1)} %bitcast.55, f32[4,256,256,5]{2,1,3,0:T(8,128)} %get-tuple-element.430, ...), kind=kOutput, calls=%fused_computation.15.clone.1 | convolution fusion | flops 342753280 | bytes 10854401 | tf_op jit(solution)/shard_map/while/body/eval_jaxpr/hgqk,khd->qhgd/dot_general | solution.py:78
  152.8 3.6 %fusion.48 = f32[4,5,256]{2,1,0:T(8,128)S(1)} fusion(f32[4,256,256,5]{2,1,3,0:T(8,128)} %get-tuple-element.430, f32[4,5,256]{2,1,0:T(8,128)S(1)} %get-tuple-element.462, pred[256,256]{0,1:T(8,128)(4,1)S(1)} %compare_and_fusion.4), kind=kLoop, calls=%fused_computation.13.clone.1 | loop fusion | flops 5237760 | bytes 5349376 | tf_op jit(solution)/shard_map/while/body/eval_jaxpr/reduce_sum | solution.py:76
  156.6 1.9 gather_fusion
  158.6 1.9 gather_fusion.1
  161.9 3.4 %fusion.46 = (f32[4,5,256]{2,1,0:T(8,128)S(1)}, f32[4,256,256,5]{2,1,3,0:T(8,128)}) fusion(pred[256,256]{0,1:T(8,128)(4,1)S(1)} %compare_and_fusion.4, bf16[256,4,128,1]{0,2,3,1:T(8,128)(2,1)S(1)} %bitcast.56, bf16[256,4,5,128]{3,0,2,1:T(8,128)(2,1)S(1)} %get-tuple-element.467), kind=kOutput, calls=%fused_computation.9.clone.1 | convolution fusion | flops 339471360 | bytes 6901760 | tf_op jit(solution)/shard_map/while/body/eval_jaxpr/qhgd,khd->hgqk/dot_general | solution.py:67
  165.4 6.2 %bitcast_add_fusion.2 = f32[256,4,5,128]{0,3,2,1:T(8,128)} fusion(f32[256,4,5,128]{0,3,2,1:T(8,128)} %get-tuple-element.450, f32[256,4,5]{0,2,1:T(8,128)S(1)} %get-tuple-element.431, pred[]{:T(512)S(6)} %compare.22, bf16[256,4,128,1]{0,2,3,1:T(8,128)(2,1)S(1)} %bitcast.55, f32[4,256,256,5]{2,1,3,0:T(8,128)} %get-tuple-element.430, ...), kind=kOutput, calls=%fused_computation.15.clone.1 | convolution fusion | flops 342753280 | bytes 10854401 | tf_op jit(solution)/shard_map/while/body/eval_jaxpr/hgqk,khd->qhgd/dot_general | solution.py:78
  171.6 3.6 %fusion.48 = f32[4,5,256]{2,1,0:T(8,128)S(1)} fusion(f32[4,256,256,5]{2,1,3,0:T(8,128)} %get-tuple-element.430, f32[4,5,256]{2,1,0:T(8,128)S(1)} %get-tuple-element.462, pred[256,256]{0,1:T(8,128)(4,1)S(1)} %compare_and_fusion.4), kind=kLoop, calls=%fused_computation.13.clone.1 | loop fusion | flops 5237760 | bytes 5349376 | tf_op jit(solution)/shard_map/while/body/eval_jaxpr/reduce_sum | solution.py:76
  175.4 1.9 gather_fusion
  177.3 1.9 gather_fusion.1
  180.7 3.4 %fusion.46 = (f32[4,5,256]{2,1,0:T(8,128)S(1)}, f32[4,256,256,5]{2,1,3,0:T(8,128)}) fusion(pred[256,256]{0,1:T(8,128)(4,1)S(1)} %compare_and_fusion.4, bf16[256,4,128,1]{0,2,3,1:T(8,128)(2,1)S(1)} %bitcast.56, bf16[256,4,5,128]{3,0,2,1:T(8,128)(2,1)S(1)} %get-tuple-element.467), kind=kOutput, calls=%fused_computation.9.clone.1 | convolution fusion | flops 339471360 | bytes 6901760 | tf_op jit(solution)/shard_map/while/body/eval_jaxpr/qhgd,khd->hgqk/dot_general | solution.py:67
  184.2 6.2 %bitcast_add_fusion.2 = f32[256,4,5,128]{0,3,2,1:T(8,128)} fusion(f32[256,4,5,128]{0,3,2,1:T(8,128)} %get-tuple-element.450, f32[256,4,5]{0,2,1:T(8,128)S(1)} %get-tuple-element.431, pred[]{:T(512)S(6)} %compare.22, bf16[256,4,128,1]{0,2,3,1:T(8,128)(2,1)S(1)} %bitcast.55, f32[4,256,256,5]{2,1,3,0:T(8,128)} %get-tuple-element.430, ...), kind=kOutput, calls=%fused_computation.15.clone.1 | convolution fusion | flops 342753280 | bytes 10854401 | tf_op jit(solution)/shard_map/while/body/eval_jaxpr/hgqk,khd->qhgd/dot_general | solution.py:78
  190.4 3.6 %fusion.48 = f32[4,5,256]{2,1,0:T(8,128)S(1)} fusion(f32[4,256,256,5]{2,1,3,0:T(8,128)} %get-tuple-element.430, f32[4,5,256]{2,1,0:T(8,128)S(1)} %get-tuple-element.462, pred[256,256]{0,1:T(8,128)(4,1)S(1)} %compare_and_fusion.4), kind=kLoop, calls=%fused_computation.13.clone.1 | loop fusion | flops 5237760 | bytes 5349376 | tf_op jit(solution)/shard_map/while/body/eval_jaxpr/reduce_sum | solution.py:76
  194.1 1.9 gather_fusion
  199.4 3.4 %fusion.46 = (f32[4,5,256]{2,1,0:T(8,128)S(1)}, f32[4,256,256,5]{2,1,3,0:T(8,128)}) fusion(pred[256,256]{0,1:T(8,128)(4,1)S(1)} %compare_and_fusion.4, bf16[256,4,128,1]{0,2,3,1:T(8,128)(2,1)S(1)} %bitcast.56, bf16[256,4,5,128]{3,0,2,1:T(8,128)(2,1)S(1)} %get-tuple-element.467), kind=kOutput, calls=%fused_computation.9.clone.1 | convolution fusion | flops 339471360 | bytes 6901760 | tf_op jit(solution)/shard_map/while/body/eval_jaxpr/qhgd,khd->hgqk/dot_general | solution.py:67
  203.0 6.2 %bitcast_add_fusion.2 = f32[256,4,5,128]{0,3,2,1:T(8,128)} fusion(f32[256,4,5,128]{0,3,2,1:T(8,128)} %get-tuple-element.450, f32[256,4,5]{0,2,1:T(8,128)S(1)} %get-tuple-element.431, pred[]{:T(512)S(6)} %compare.22, bf16[256,4,128,1]{0,2,3,1:T(8,128)(2,1)S(1)} %bitcast.55, f32[4,256,256,5]{2,1,3,0:T(8,128)} %get-tuple-element.430, ...), kind=kOutput, calls=%fused_computation.15.clone.1 | convolution fusion | flops 342753280 | bytes 10854401 | tf_op jit(solution)/shard_map/while/body/eval_jaxpr/hgqk,khd->qhgd/dot_general | solution.py:78
  209.1 3.6 %fusion.48 = f32[4,5,256]{2,1,0:T(8,128)S(1)} fusion(f32[4,256,256,5]{2,1,3,0:T(8,128)} %get-tuple-element.430, f32[4,5,256]{2,1,0:T(8,128)S(1)} %get-tuple-element.462, pred[256,256]{0,1:T(8,128)(4,1)S(1)} %compare_and_fusion.4), kind=kLoop, calls=%fused_computation.13.clone.1 | loop fusion | flops 5237760 | bytes 5349376 | tf_op jit(solution)/shard_map/while/body/eval_jaxpr/reduce_sum | solution.py:76
  214.9 1.9 gather_fusion.1
  218.2 3.4 %fusion.46 = (f32[4,5,256]{2,1,0:T(8,128)S(1)}, f32[4,256,256,5]{2,1,3,0:T(8,128)}) fusion(pred[256,256]{0,1:T(8,128)(4,1)S(1)} %compare_and_fusion.4, bf16[256,4,128,1]{0,2,3,1:T(8,128)(2,1)S(1)} %bitcast.56, bf16[256,4,5,128]{3,0,2,1:T(8,128)(2,1)S(1)} %get-tuple-element.467), kind=kOutput, calls=%fused_computation.9.clone.1 | convolution fusion | flops 339471360 | bytes 6901760 | tf_op jit(solution)/shard_map/while/body/eval_jaxpr/qhgd,khd->hgqk/dot_general | solution.py:67
  221.7 6.2 %bitcast_add_fusion.2 = f32[256,4,5,128]{0,3,2,1:T(8,128)} fusion(f32[256,4,5,128]{0,3,2,1:T(8,128)} %get-tuple-element.450, f32[256,4,5]{0,2,1:T(8,128)S(1)} %get-tuple-element.431, pred[]{:T(512)S(6)} %compare.22, bf16[256,4,128,1]{0,2,3,1:T(8,128)(2,1)S(1)} %bitcast.55, f32[4,256,256,5]{2,1,3,0:T(8,128)} %get-tuple-element.430, ...), kind=kOutput, calls=%fused_computation.15.clone.1 | convolution fusion | flops 342753280 | bytes 10854401 | tf_op jit(solution)/shard_map/while/body/eval_jaxpr/hgqk,khd->qhgd/dot_general | solution.py:78
  227.9 3.6 %fusion.48 = f32[4,5,256]{2,1,0:T(8,128)S(1)} fusion(f32[4,256,256,5]{2,1,3,0:T(8,128)} %get-tuple-element.430, f32[4,5,256]{2,1,0:T(8,128)S(1)} %get-tuple-element.462, pred[256,256]{0,1:T(8,128)(4,1)S(1)} %compare_and_fusion.4), kind=kLoop, calls=%fused_computation.13.clone.1 | loop fusion | flops 5237760 | bytes 5349376 | tf_op jit(solution)/shard_map/while/body/eval_jaxpr/reduce_sum | solution.py:76
  237.0 3.4 %fusion.46 = (f32[4,5,256]{2,1,0:T(8,128)S(1)}, f32[4,256,256,5]{2,1,3,0:T(8,128)}) fusion(pred[256,256]{0,1:T(8,128)(4,1)S(1)} %compare_and_fusion.4, bf16[256,4,128,1]{0,2,3,1:T(8,128)(2,1)S(1)} %bitcast.56, bf16[256,4,5,128]{3,0,2,1:T(8,128)(2,1)S(1)} %get-tuple-element.467), kind=kOutput, calls=%fused_computation.9.clone.1 | convolution fusion | flops 339471360 | bytes 6901760 | tf_op jit(solution)/shard_map/while/body/eval_jaxpr/qhgd,khd->hgqk/dot_general | solution.py:67
  240.5 6.2 %bitcast_add_fusion.2 = f32[256,4,5,128]{0,3,2,1:T(8,128)} fusion(f32[256,4,5,128]{0,3,2,1:T(8,128)} %get-tuple-element.450, f32[256,4,5]{0,2,1:T(8,128)S(1)} %get-tuple-element.431, pred[]{:T(512)S(6)} %compare.22, bf16[256,4,128,1]{0,2,3,1:T(8,128)(2,1)S(1)} %bitcast.55, f32[4,256,256,5]{2,1,3,0:T(8,128)} %get-tuple-element.430, ...), kind=kOutput, calls=%fused_computation.15.clone.1 | convolution fusion | flops 342753280 | bytes 10854401 | tf_op jit(solution)/shard_map/while/body/eval_jaxpr/hgqk,khd->qhgd/dot_general | solution.py:78
  246.7 3.6 %fusion.48 = f32[4,5,256]{2,1,0:T(8,128)S(1)} fusion(f32[4,256,256,5]{2,1,3,0:T(8,128)} %get-tuple-element.430, f32[4,5,256]{2,1,0:T(8,128)S(1)} %get-tuple-element.462, pred[256,256]{0,1:T(8,128)(4,1)S(1)} %compare_and_fusion.4), kind=kLoop, calls=%fused_computation.13.clone.1 | loop fusion | flops 5237760 | bytes 5349376 | tf_op jit(solution)/shard_map/while/body/eval_jaxpr/reduce_sum | solution.py:76
  250.3 2.0 divide_convert_fusion
  (134 shorter events, 27.2 us)
Async XLA Ops:
  6.5 40.2 %copy-start = (bf16[256,2560]{1,0:T(8,128)(2,1)S(1)}, bf16[256,2560]{1,0:T(8,128)(2,1)}, u32[]{:S(2)}) copy-start(bf16[256,2560]{1,0:T(8,128)(2,1)} %param.8) | copy-start | bytes 3932164
  6.5 94.4 %all-gather.2.cloned.1.call-start = ((), (), s32[]{:S(2)}) async-start(), calls=%async_computation.2 | async-start | bytes 4718592 | tf_op jit(solution)/shard_map/all_gather | solution.py:46
  49.4 9.6 %copy-start.1 = (s32[256]{0:T(256)S(1)}, s32[256]{0:T(256)}, u32[]{:S(2)}) copy-start(s32[256]{0:T(256)} %param.11) | copy-start | bytes 3076
  52.5 40.5 %all-to-all-start.1 = ((bf16[64,4,2560]{2,1,0:T(4,128)(2,1)}), bf16[64,4,2560]{2,1,0:T(4,128)(2,1)S(1)}, u32[]{:S(2)}, u32[]{:S(2)}) async-start(bf16[64,4,2560]{2,1,0:T(4,128)(2,1)} %broadcast_select_fusion.1), calls=%async_computation.1 | async-start | bytes 2621440 | tf_op jit(solution)/shard_map/all_to_all | solution.py:27
Sparse Core Ops, SparseCore 0:
  46.9 54.0 all-gather.1
where the time goes:
time: 262 us; the launch traced here: 261 us
  matrix products  75.4 us (29%)
  local copies, waits for them, and re-layouts  57.5 us (22%)
  other arithmetic  39.7 us (15%)
  waiting for transfers between devices  35.4 us (14%)
  blocking collectives  32 us (12%)
  between operations  13.5 us (5%)
  starting transfers between devices  6.29 us (2%)
    dot_general x8, matrix products, one_block(): jnp.einsum('hgqk,khd->qhgd', weights, value_head_rows, preferred_element_...  48.5 us
    all_to_all x1, blocking collectives, local(): lax.all_to_all(outgoing[1], 'ctx', split_axis=0, concat_axis=0, tiled=True)  32 us
    all_to_all x1, waiting for transfers between devices, local(): lax.all_to_all(outgoing[0], 'ctx', split_axis=0, concat_axis=0, tiled=True)  31.9 us
    reduce_sum x8, other arithmetic, one_block(): running_sum = running_sum * factor + jnp.sum(exponent, axis=-1)  28.5 us
    dot_general x8, matrix products, one_block(): jnp.einsum('qhgd,khd->hgqk', head_grouped, key_head_rows, preferred_eleme...  26.9 us
    gather x8, local copies, waits for them, and re-layouts, one_block(): key_document = jnp.take(row_document, local_rows)  15.5 us
    gather x8, local copies, waits for them, and re-layouts, one_block(): jnp.take(base_position, local_rows) + where_ids // count_of_rows  15.5 us
    slice x8, local copies, waits for them, and re-layouts, one_block(): rows_per_block[:, KEY_VALUE_HEADS * HEAD_SIZE:]  8.56 us
  transfers between devices with their start and end apart: 2, of which 2 were waited for; matrix products, arithmetic and copies ran while one was open for 5% of the time, Pallas kernels for 0%

commit v1 on v0

v1 whole, which is shorter than its diff:
```python
import math

import jax
import jax.numpy as jnp
from jax import lax
from jax.experimental import pallas as pl
from jax.experimental.pallas import tpu as pltpu
from jax.sharding import PartitionSpec as P

QUERY_HEADS = 20
KEY_VALUE_HEADS = 4
HEAD_SIZE = 128
SHARED = QUERY_HEADS // KEY_VALUE_HEADS
X, Z, CORES, G = 4, 8, 2, 8
N_CTX = X * Z * CORES
UNITS = 4
ROWS = N_CTX * UNITS
MESH = pl.DeviceIdType.MESH
F32, BF16 = jnp.float32, jnp.bfloat16
NEGATIVE = -1e30
EXPONENT = math.log2(math.e) / math.sqrt(HEAD_SIZE)
SLOT = {0: 0, 1: 1, 7: 2, 2: 3, 6: 4, 3: 5, 5: 6, 4: 7}
REL = {slot: rel for rel, slot in SLOT.items()}
Q_TILES = QUERY_HEADS // 4


def z_offset(i):
    odd = i % 2
    return odd * ((i + 1) // 2) + (1 - odd) * ((8 - i // 2) % 8)


def kernel(
    slot_ref, doc_ref, q_hbm, kv_hbm, out_hbm,
    q_in, kv_in, send, kv_got, q_got, gathered, q_heads, out_v,
    stage, out_stage, bias_full, bias_a, bias_b,
    in_sem, out_sem, own_sem, send_sem, kv_sem, q_sem, ring_send, ring_recv,
):
    ctx, grp = lax.axis_index("ctx"), lax.axis_index("grp")
    x, z, core = ctx // (Z * CORES), (ctx // CORES) % Z, ctx % CORES
    xk = x * CORES + core

    def peer(n):
        i, w = n // 8, n % 8
        return (((x + w // 2) % X) * Z + (z + z_offset(i)) % Z) * CORES + (core + w % 2) % CORES

    load_kv = pltpu.make_async_copy(kv_hbm, kv_in, in_sem.at[0])
    load_q = pltpu.make_async_copy(q_hbm, q_in, in_sem.at[1])
    load_kv.start()
    load_q.start()

    barrier = pltpu.get_barrier_semaphore()

    def greet(n, carry):
        pl.semaphore_signal(barrier, inc=1, device_id=(peer(n), grp), device_id_type=MESH)
        return carry

    lax.fori_loop(1, N_CTX, greet, 0)
    right, left = (ctx, (grp + 1) % G), (ctx, (grp + G - 1) % G)
    for side in (right, left):
        pl.semaphore_signal(barrier, inc=1, device_id=side, device_id_type=MESH)

    place = lax.broadcasted_iota(jnp.int32, (ROWS, ROWS), 0)
    wanted = (place % N_CTX) * UNITS + place // N_CTX
    permute = jnp.where(slot_ref[...] == wanted, 1.0, 0.0).astype(BF16)

    def lay_out(tile, values):
        part = stage.at[tile % 2]
        for j in range(4):
            for k in range(UNITS):
                part[pl.ds(j * 4 + k, N_CTX, stride=16), :] = values[j][k * N_CTX : (k + 1) * N_CTX]
        send[tile] = part[...].reshape(N_CTX, 16, HEAD_SIZE).astype(BF16)

    def kv_copy(tile, n, place, sem):
        t = peer(n)
        return pltpu.make_async_remote_copy(
            src_ref=send.at[tile, t], dst_ref=kv_got.at[tile, n // 8 * 8 + xk],
            send_sem=send_sem.at[tile], recv_sem=sem, device_id=(t, grp), device_id_type=MESH,
        )

    def send_kv(tile):
        pltpu.make_async_copy(send.at[tile, ctx], kv_got.at[tile, xk], own_sem.at[tile]).start()
        for p in range(4):
            def go(n, carry, p=p):
                kv_copy(tile, n, None, kv_sem.at[tile, p]).start()
                return carry

            lax.fori_loop(max(1, 16 * p), 16 * p + 16, go, 0)

    def send_q(tile):
        pltpu.make_async_copy(send.at[tile + 2, ctx], q_got.at[tile, ctx], own_sem.at[tile + 2]).start()

        def go(n, carry):
            t = peer(n)
            pltpu.make_async_remote_copy(
                src_ref=send.at[tile + 2, t], dst_ref=q_got.at[tile, ctx],
                send_sem=send_sem.at[tile + 2], recv_sem=q_sem.at[tile], device_id=(t, grp), device_id_type=MESH,
            ).start()
            return carry

        lax.fori_loop(1, N_CTX, go, 0)

    def prepare_q(tile):
        y = jnp.dot(permute, q_in[:, tile * 512 : tile * 512 + 512], preferred_element_type=F32)
        lay_out(tile + 2, [y[:, j * 128 : j * 128 + 128] for j in range(4)])
        send_q(tile)

    def prepare_kv(tile):
        k2 = jnp.dot(permute, kv_in[:, tile * 256 : tile * 256 + 256], preferred_element_type=F32)
        v2 = jnp.dot(permute, kv_in[:, 512 + tile * 256 : 512 + tile * 256 + 256], preferred_element_type=F32)
        lay_out(tile, [k2[:, :128], v2[:, :128], k2[:, 128:], v2[:, 128:]])

    def ring(way, pair, p, step):
        rel_from, rel_to = ((-step) % G, (-step - 1) % G) if way == 0 else (step, step + 1)
        return pltpu.make_async_remote_copy(
            src_ref=gathered.at[pair, p, SLOT[rel_from]], dst_ref=gathered.at[pair, p, SLOT[rel_to]],
            send_sem=ring_send.at[way, pair, p, step], recv_sem=ring_recv.at[way, pair, p, step],
            device_id=right if way == 0 else left, device_id_type=MESH,
        )

    def ring_has(way, p, step):
        return step < 3 or (p < 2) == (way == 0)

    def open_ring(pair, p):
        n = 15 if p == 0 else 16
        piece = kv_got.at[pair, pl.ds(0, n)]
        if p == 0:
            own = kv_got.at[pair, 0]
            pltpu.make_async_copy(own, own, own_sem.at[pair]).wait()
        pltpu.make_async_copy(piece, piece, kv_sem.at[pair, p]).wait()
        part = stage.at[p % 2]
        part[0:256, :] = kv_got[pair, 16 * p : 16 * p + 16].reshape(256, HEAD_SIZE).astype(F32)
        for j in range(4):
            for k in range(UNITS):
                gathered[pair, p, 0, j, k] = part[pl.ds(j * 4 + k, 16, stride=16), :].astype(BF16)
        for way in range(2):
            ring(way, pair, p, 0).start()

    def pass_on(pair, p, step):
        for way in range(2):
            ring(way, pair, p, step - 1).wait_recv()
            if ring_has(way, p, step):
                ring(way, pair, p, step).start()

    def last_of_ring(pair, p):
        ring(0 if p < 2 else 1, pair, p, 3).wait_recv()

    def take_q(tile):
        own = q_got.at[tile, 0]
        pltpu.make_async_copy(own, own, own_sem.at[tile + 2]).wait()
        piece = q_got.at[tile, pl.ds(0, N_CTX - 1)]
        pltpu.make_async_copy(piece, piece, q_sem.at[tile]).wait()
        part = stage.at[tile % 2]
        part[...] = q_got[tile].reshape(N_CTX * 16, HEAD_SIZE).astype(F32)
        for j in range(4):
            for k in range(UNITS):
                q_heads[tile * 4 + j, k] = part[pl.ds(j * 4 + k, N_CTX, stride=16), :].astype(BF16)

    def fill_bias(ref, low, high):
        wide = high - low
        width = 64 * wide
        docs = [
            jnp.sum(jnp.where(slot_ref[...] == ctx * UNITS + k, doc_ref[...], 0).astype(F32), axis=1, keepdims=True)
            for k in range(UNITS)
        ]
        at = lax.broadcasted_iota(jnp.int32, (N_CTX, width), 1)
        p, place, source = at // (16 * wide), (at // 16) % wide, at % 16
        rel = jnp.zeros_like(at)
        for s in range(low, high):
            rel = jnp.where(place == s - low, REL[s], rel)
        xk_key, i = source % 8, 2 * p + source // 8
        z_key = (z - z_offset(i) + Z) % Z
        key = ((xk_key // 2 * Z + z_key) * CORES + xk_key % 2) * G + (grp + rel) % G
        query = lax.broadcasted_iota(jnp.int32, (N_CTX, width), 0) * G + grp
        causal = jnp.where(key <= query, 0.0, NEGATIVE)
        for k in range(UNITS):
            for k2 in range(k):
                ref[k, :, k2 * width : (k2 + 1) * width] = jnp.broadcast_to(
                    jnp.where(docs[k2] == docs[k], 0.0, NEGATIVE), (N_CTX, width)
                )
            ref[k, :, k * width : (k + 1) * width] = causal

    def attend(h, stages):
        pair, jk = h // 2, h % 2 * 2
        for k in range(UNITS):
            q = q_heads[h * SHARED : (h + 1) * SHARED, k].reshape(SHARED * N_CTX, HEAD_SIZE)
            top = total = None
            for low, high, bias in stages:
                width = 64 * (high - low)
                count = width * (k + 1)

                def rows(j, low=low, high=high, width=width):
                    return jnp.concatenate(
                        [gathered[pair, :, low:high, j, k2].reshape(width, HEAD_SIZE) for k2 in range(k + 1)], axis=0
                    )

                s = lax.dot_general(q, rows(jk), (((1,), (1,)), ((), ())), preferred_element_type=F32)
                s = s.reshape(SHARED, N_CTX, count) + bias[k, :, 0:count][None]
                s = s.reshape(SHARED * N_CTX, count)
                new_top = jnp.max(s, axis=1, keepdims=True)
                if top is not None:
                    new_top = jnp.maximum(top, new_top)
                weights = jnp.exp2((s - new_top) * EXPONENT).astype(BF16)
                values = jnp.concatenate([rows(jk + 1), jnp.ones((count, HEAD_SIZE), BF16)], axis=1)
                part = jnp.dot(weights, values, preferred_element_type=F32)
                total = part if top is None else total * jnp.exp2((top - new_top) * EXPONENT) + part
                top = new_top
            result = total[:, :HEAD_SIZE] / total[:, HEAD_SIZE:]
            for i in range(SHARED):
                out_stage[i, pl.ds(k, N_CTX, stride=UNITS), :] = result[i * N_CTX : (i + 1) * N_CTX]
        for i in range(SHARED):
            col = (h * SHARED + i) * HEAD_SIZE
            out_v[:, col : col + HEAD_SIZE] = out_stage[i].astype(BF16)
        store(h).start()

    def store(h):
        cols = pl.ds(h * SHARED * HEAD_SIZE, SHARED * HEAD_SIZE)
        return pltpu.make_async_copy(out_v.at[:, cols], out_hbm.at[:, cols], out_sem.at[h])

    load_kv.wait()
    prepare_kv(0)
    pl.semaphore_wait(barrier, N_CTX - 1 + 2)
    send_kv(0)
    prepare_kv(1)
    send_kv(1)
    load_q.wait()
    for tile in range(4):
        prepare_q(tile)
        open_ring(0, tile)
    prepare_q(4)
    fill_bias(bias_full, 0, G)
    fill_bias(bias_a, 0, 4)
    fill_bias(bias_b, 4, G)
    for p in range(4):
        pass_on(0, p, 1)
    for p in range(4):
        pass_on(0, p, 2)
    for p in range(4):
        pass_on(0, p, 3)
        open_ring(1, p)
    for p in range(4):
        last_of_ring(0, p)
    take_q(0)
    take_q(1)
    attend(0, [(0, G, bias_full)])
    for p in range(4):
        pass_on(1, p, 1)
    take_q(2)
    attend(1, [(0, G, bias_full)])
    for p in range(4):
        pass_on(1, p, 2)
    take_q(3)
    for p in range(4):
        pass_on(1, p, 3)
    take_q(4)
    for p in range(4):
        last_of_ring(1, p)
    attend(2, [(0, G, bias_full)])
    attend(3, [(0, G, bias_full)])

    for h in range(KEY_VALUE_HEADS):
        store(h).wait()
    for tile in range(2 + Q_TILES):
        piece = send.at[tile, pl.ds(0, N_CTX - 1)]
        pltpu.make_async_copy(piece, piece, send_sem.at[tile]).wait()
    for way in range(2):
        for pair in range(2):
            for p in range(4):
                for step in range(4):
                    if ring_has(way, p, step):
                        ring(way, pair, p, step).wait_send()


def local(queries, key_value_rows, unit_slot, unit_doc):
    dma = pltpu.SemaphoreType.DMA
    tiles = 2 + Q_TILES
    any_spec = pl.BlockSpec(memory_space=pl.ANY)
    vmem_spec = pl.BlockSpec(memory_space=pltpu.VMEM)
    return pl.pallas_call(
        kernel,
        name="repacked_attention",
        out_shape=jax.ShapeDtypeStruct(queries.shape, BF16),
        in_specs=[vmem_spec, vmem_spec, any_spec, any_spec],
        out_specs=any_spec,
        scratch_shapes=[
            pltpu.VMEM(queries.shape, BF16),
            pltpu.VMEM(key_value_rows.shape, BF16),
            pltpu.VMEM((tiles, N_CTX, 16, HEAD_SIZE), BF16),
            pltpu.VMEM((2, N_CTX, 16, HEAD_SIZE), BF16),
            pltpu.VMEM((Q_TILES, N_CTX, 16, HEAD_SIZE), BF16),
            pltpu.VMEM((2, 4, G, 4, UNITS, 16, HEAD_SIZE), BF16),
            pltpu.VMEM((QUERY_HEADS, UNITS, N_CTX, HEAD_SIZE), BF16),
            pltpu.VMEM(queries.shape, BF16),
            pltpu.VMEM((2, N_CTX * 16, HEAD_SIZE), F32),
            pltpu.VMEM((SHARED, ROWS, HEAD_SIZE), F32),
            pltpu.VMEM((UNITS, N_CTX, 64 * G * UNITS), F32),
            pltpu.VMEM((UNITS, N_CTX, 64 * 4 * UNITS), F32),
            pltpu.VMEM((UNITS, N_CTX, 64 * 4 * UNITS), F32),
            dma((2,)),
            dma((KEY_VALUE_HEADS,)),
            dma((tiles,)),
            dma((tiles,)),
            dma((2, 4)),
            dma((Q_TILES,)),
            dma((2, 2, 4, 4)),
            dma((2, 2, 4, 4)),
        ],
        compiler_params=pltpu.CompilerParams(
            collective_id=0, has_side_effects=True, vmem_limit_bytes=56 * 2**20
        ),
        cost_estimate=pl.CostEstimate(flops=5 * 10**9, bytes_accessed=4 * 10**6, transcendentals=6 * 10**6),
    )(unit_slot.reshape(1, -1), unit_doc.reshape(1, -1), queries, key_value_rows)


def solution(mesh):
    in_specs = (P(("ctx", "grp"), None), P(("ctx", "grp"), None), P(), P())
    out_specs = P(("ctx", "grp"), None)
    return jax.shard_map(local, mesh=mesh, in_specs=in_specs, out_specs=out_specs, check_vma=False)
```

time: 262 us -> 91.7 us (0.35)
  the two profiles are of different devices: /device:TPU:1 before, /device:TPU:24 now
where the time goes in v1:
time: 91.7 us; the launch traced here: 91.5 us
  Pallas kernels  89.1 us (97%)
  local copies, waits for them, and re-layouts  2.46 us (3%)
    pallas_call x1, Pallas kernels, local(): pl.pallas_call(kernel, name='repacked_attention', out_shape=jax.ShapeDtyp...  89.1 us
    unnamed x1, local copies, waits for them, and re-layouts  2.46 us

profile of v1, /device:TPU:24, one launch (start us, length us, event | category | flops | bytes accessed | tf_op | source)
XLA Modules:
  0.0 91.5 jit_solution(9670855533860499160)
XLA Ops:
  0.0 89.1 %repacked_attention.1 = bf16[256,2560]{1,0:T(8,128)(2,1)} custom-call(s32[1,256]{1,0:T(1,128)} %bitcast.2, s32[1,256]{1,0:T(1,128)} %bitcast.3, bf16[256,2560]{1,0:T(8,128)(2,1)} %q_hbm.1, bf16[256,1024]{1,0:T(8,128)(2,1)} %kv_hbm.1), custom_call_target="tpu_custom_call" | custom-call | flops 5000000000 | bytes 4000000 | tf_op jit(solution)/shard_map/repacked_attention/pallas_call | solution.py:278
  89.1 2.5 %copy.6 = bf16[256,2560]{1,0:T(8,128)(2,1)} copy(bf16[256,2560]{1,0:T(8,128)(2,1)} %repacked_attention.1) | data formatting | bytes 2621440

commit v2 on v1

--- a/solution.py
+++ b/solution.py
@@ -22,6 +22,7 @@
 SLOT = {0: 0, 1: 1, 7: 2, 2: 3, 6: 4, 3: 5, 5: 6, 4: 7}
 REL = {slot: rel for rel, slot in SLOT.items()}
 Q_TILES = QUERY_HEADS // 4
+LEAD = 4
 
 
 def z_offset(i):
@@ -30,10 +31,10 @@
 
 
 def kernel(
-    slot_ref, doc_ref, q_hbm, kv_hbm, out_hbm,
-    q_in, kv_in, send, kv_got, q_got, gathered, q_heads, out_v,
-    stage, out_stage, bias_full, bias_a, bias_b,
-    in_sem, out_sem, own_sem, send_sem, kv_sem, q_sem, ring_send, ring_recv,
+    slot_ref, doc_ref, q_hbm, kv_hbm, out_ref,
+    q_in, kv_in, send, kv_got, q_got, gathered, q_heads,
+    stage, out_stage, bias_full, bias_a, bias_b, bias_c,
+    in_sem, own_sem, send_sem, kv_sem, q_sem, ring_send, ring_recv,
 ):
     ctx, grp = lax.axis_index("ctx"), lax.axis_index("grp")
     x, z, core = ctx // (Z * CORES), (ctx // CORES) % Z, ctx % CORES
@@ -70,39 +71,37 @@
                 part[pl.ds(j * 4 + k, N_CTX, stride=16), :] = values[j][k * N_CTX : (k + 1) * N_CTX]
         send[tile] = part[...].reshape(N_CTX, 16, HEAD_SIZE).astype(BF16)
 
-    def kv_copy(tile, n, place, sem):
-        t = peer(n)
-        return pltpu.make_async_remote_copy(
-            src_ref=send.at[tile, t], dst_ref=kv_got.at[tile, n // 8 * 8 + xk],
-            send_sem=send_sem.at[tile], recv_sem=sem, device_id=(t, grp), device_id_type=MESH,
-        )
-
-    def send_kv(tile):
-        pltpu.make_async_copy(send.at[tile, ctx], kv_got.at[tile, xk], own_sem.at[tile]).start()
-        for p in range(4):
-            def go(n, carry, p=p):
-                kv_copy(tile, n, None, kv_sem.at[tile, p]).start()
-                return carry
-
-            lax.fori_loop(max(1, 16 * p), 16 * p + 16, go, 0)
-
-    def send_q(tile):
-        pltpu.make_async_copy(send.at[tile + 2, ctx], q_got.at[tile, ctx], own_sem.at[tile + 2]).start()
+    def send_kv(tile, p):
+        if p == 0:
+            pltpu.make_async_copy(send.at[tile, ctx], kv_got.at[tile, xk], own_sem.at[tile]).start()
 
         def go(n, carry):
             t = peer(n)
+            pltpu.make_async_remote_copy(
+                src_ref=send.at[tile, t], dst_ref=kv_got.at[tile, n // 8 * 8 + xk],
+                send_sem=send_sem.at[tile], recv_sem=kv_sem.at[tile, p], device_id=(t, grp), device_id_type=MESH,
+            ).start()
+            return carry
+
+        lax.fori_loop(max(1, 16 * p), 16 * p + 16, go, 0)
+
+    def send_q(tile, part):
+        if part == 0:
+            pltpu.make_async_copy(send.at[tile + 2, ctx], q_got.at[tile, ctx], own_sem.at[tile + 2]).start()
+
+        def go(m, carry):
+            t = peer(m // 2 * 8 + part * 2 + m % 2)
             pltpu.make_async_remote_copy(
                 src_ref=send.at[tile + 2, t], dst_ref=q_got.at[tile, ctx],
                 send_sem=send_sem.at[tile + 2], recv_sem=q_sem.at[tile], device_id=(t, grp), device_id_type=MESH,
             ).start()
             return carry
 
-        lax.fori_loop(1, N_CTX, go, 0)
+        lax.fori_loop(1 if part == 0 else 0, 16, go, 0)
 
     def prepare_q(tile):
         y = jnp.dot(permute, q_in[:, tile * 512 : tile * 512 + 512], preferred_element_type=F32)
         lay_out(tile + 2, [y[:, j * 128 : j * 128 + 128] for j in range(4)])
-        send_q(tile)
 
     def prepare_kv(tile):
         k2 = jnp.dot(permute, kv_in[:, tile * 256 : tile * 256 + 256], preferred_element_type=F32)
@@ -179,86 +178,118 @@
                 )
             ref[k, :, k * width : (k + 1) * width] = causal
 
-    def attend(h, stages):
+    def attend(h, k, low, high, bias, state=None):
         pair, jk = h // 2, h % 2 * 2
-        for k in range(UNITS):
-            q = q_heads[h * SHARED : (h + 1) * SHARED, k].reshape(SHARED * N_CTX, HEAD_SIZE)
-            top = total = None
-            for low, high, bias in stages:
-                width = 64 * (high - low)
-                count = width * (k + 1)
-
-                def rows(j, low=low, high=high, width=width):
-                    return jnp.concatenate(
-                        [gathered[pair, :, low:high, j, k2].reshape(width, HEAD_SIZE) for k2 in range(k + 1)], axis=0
-                    )
-
-                s = lax.dot_general(q, rows(jk), (((1,), (1,)), ((), ())), preferred_element_type=F32)
-                s = s.reshape(SHARED, N_CTX, count) + bias[k, :, 0:count][None]
-                s = s.reshape(SHARED * N_CTX, count)
-                new_top = jnp.max(s, axis=1, keepdims=True)
-                if top is not None:
-                    new_top = jnp.maximum(top, new_top)
-                weights = jnp.exp2((s - new_top) * EXPONENT).astype(BF16)
-                values = jnp.concatenate([rows(jk + 1), jnp.ones((count, HEAD_SIZE), BF16)], axis=1)
-                part = jnp.dot(weights, values, preferred_element_type=F32)
-                total = part if top is None else total * jnp.exp2((top - new_top) * EXPONENT) + part
-                top = new_top
-            result = total[:, :HEAD_SIZE] / total[:, HEAD_SIZE:]
+        width = 64 * (high - low)
+        q = q_heads[h * SHARED : (h + 1) * SHARED, k].reshape(SHARED * N_CTX, HEAD_SIZE)
+        group = max(1, 512 // width)
+        for last in range(k, -1, -group):
+            units = range(max(0, last - group + 1), last + 1)
+            count = width * len(units)
+
+            def rows(j):
+                return jnp.concatenate([gathered[pair, :, low:high, j, k2].reshape(width, HEAD_SIZE) for k2 in units], axis=0)
+
+            s = lax.dot_general(q, rows(jk), (((1,), (1,)), ((), ())), preferred_element_type=F32)
+            s = s.reshape(SHARED, N_CTX, count) + bias[k, :, units[0] * width : units[0] * width + count][None]
+            s = s.reshape(SHARED * N_CTX, count)
+            top = jnp.max(s, axis=1, keepdims=True)
+            if state is not None:
+                top = jnp.maximum(top, state[0])
+            weights = jnp.exp2((s - top) * EXPONENT).astype(BF16)
+            values = jnp.concatenate([rows(jk + 1), jnp.ones((count, HEAD_SIZE), BF16)], axis=1)
+            total = jnp.dot(weights, values, preferred_element_type=F32)
+            if state is not None:
+                total = total + state[1] * jnp.exp2((state[0] - top) * EXPONENT)
+            state = top, total
+        return state
+
+    def finish(h, k, state):
+        total = state[1]
+        result = total[:, :HEAD_SIZE] / total[:, HEAD_SIZE:]
+        for i in range(SHARED):
+            out_stage[i, pl.ds(k, N_CTX, stride=UNITS), :] = result[i * N_CTX : (i + 1) * N_CTX]
+        if k == UNITS - 1:
             for i in range(SHARED):
-                out_stage[i, pl.ds(k, N_CTX, stride=UNITS), :] = result[i * N_CTX : (i + 1) * N_CTX]
-        for i in range(SHARED):
-            col = (h * SHARED + i) * HEAD_SIZE
-            out_v[:, col : col + HEAD_SIZE] = out_stage[i].astype(BF16)
-        store(h).start()
-
-    def store(h):
-        cols = pl.ds(h * SHARED * HEAD_SIZE, SHARED * HEAD_SIZE)
-        return pltpu.make_async_copy(out_v.at[:, cols], out_hbm.at[:, cols], out_sem.at[h])
+                col = (h * SHARED + i) * HEAD_SIZE
+                out_ref[:, col : col + HEAD_SIZE] = out_stage[i].astype(BF16)
+
+    parts = [(tile, p) for tile in range(2 + Q_TILES) for p in range(4)]
+    issued = [0]
+
+    def issue(count):
+        while issued[0] < min(count, len(parts)):
+            tile, p = parts[issued[0]]
+            issued[0] += 1
+            if tile < 2:
+                send_kv(tile, p)
+            else:
+                if p == 0 and tile >= 4:
+                    prepare_q(tile - 2)
+                send_q(tile - 2, p)
+
+    def run(events):
+        for pair, p, step in events:
+            if step == 0:
+                open_ring(pair, p)
+            elif step < 4:
+                pass_on(pair, p, step)
+            else:
+                last_of_ring(pair, p)
+                continue
+            issue(issued[0] + 1)
 
     load_kv.wait()
     prepare_kv(0)
+    prepare_kv(1)
+    load_q.wait()
+    prepare_q(0)
+    prepare_q(1)
     pl.semaphore_wait(barrier, N_CTX - 1 + 2)
-    send_kv(0)
-    prepare_kv(1)
-    send_kv(1)
-    load_q.wait()
-    for tile in range(4):
-        prepare_q(tile)
-        open_ring(0, tile)
-    prepare_q(4)
+    issue(LEAD)
+    run([(0, 0, 0), (0, 1, 0), (0, 0, 1), (0, 2, 0), (0, 1, 1), (0, 3, 0), (0, 2, 1), (0, 0, 2), (0, 3, 1), (0, 1, 2)])
+    run([(1, 0, 0), (0, 2, 2), (0, 0, 3), (0, 3, 2), (0, 1, 3), (1, 1, 0), (1, 2, 0), (0, 2, 3), (0, 3, 3), (1, 3, 0)])
     fill_bias(bias_full, 0, G)
     fill_bias(bias_a, 0, 4)
-    fill_bias(bias_b, 4, G)
-    for p in range(4):
-        pass_on(0, p, 1)
-    for p in range(4):
-        pass_on(0, p, 2)
-    for p in range(4):
-        pass_on(0, p, 3)
-        open_ring(1, p)
-    for p in range(4):
-        last_of_ring(0, p)
+    fill_bias(bias_b, 4, 6)
+    fill_bias(bias_c, 6, G)
+    run([(1, 0, 1), (1, 1, 1)])
+    run([(0, p, 4) for p in range(4)])
     take_q(0)
     take_q(1)
-    attend(0, [(0, G, bias_full)])
-    for p in range(4):
-        pass_on(1, p, 1)
+    finish(0, 0, attend(0, 0, 0, G, bias_full))
+    finish(0, 1, attend(0, 1, 0, G, bias_full))
+    run([(1, 2, 1)])
+    finish(0, 2, attend(0, 2, 0, G, bias_full))
+    run([(1, 3, 1)])
+    finish(0, 3, attend(0, 3, 0, G, bias_full))
+    run([(1, 0, 2), (1, 1, 2)])
+    issue(len(parts))
     take_q(2)
-    attend(1, [(0, G, bias_full)])
-    for p in range(4):
-        pass_on(1, p, 2)
+    finish(1, 0, attend(1, 0, 0, G, bias_full))
+    finish(1, 1, attend(1, 1, 0, G, bias_full))
+    run([(1, 2, 2)])
+    finish(1, 2, attend(1, 2, 0, G, bias_full))
+    run([(1, 3, 2)])
+    finish(1, 3, attend(1, 3, 0, G, bias_full))
+    run([(1, 0, 3), (1, 2, 3)])
     take_q(3)
-    for p in range(4):
-        pass_on(1, p, 3)
+    early = {}
+    for k in range(UNITS):
+        early[2, k] = attend(2, k, 0, 4, bias_a)
+    run([(1, 1, 3), (1, 3, 3)])
+    for k in range(UNITS):
+        early[2, k] = attend(2, k, 4, 6, bias_b, early[2, k])
     take_q(4)
-    for p in range(4):
-        last_of_ring(1, p)
-    attend(2, [(0, G, bias_full)])
-    attend(3, [(0, G, bias_full)])
-
-    for h in range(KEY_VALUE_HEADS):
-        store(h).wait()
+    for k in range(UNITS):
+        early[3, k] = attend(3, k, 0, 4, bias_a)
+    for k in range(UNITS):
+        early[3, k] = attend(3, k, 4, 6, bias_b, early[3, k])
+    run([(1, p, 4) for p in range(4)])
+    for h in (2, 3):
+        for k in range(UNITS):
+            finish(h, k, attend(h, k, 6, G, bias_c, early[h, k]))
+
     for tile in range(2 + Q_TILES):
         piece = send.at[tile, pl.ds(0, N_CTX - 1)]
         pltpu.make_async_copy(piece, piece, send_sem.at[tile]).wait()
@@ -278,9 +309,9 @@
     return pl.pallas_call(
         kernel,
         name="repacked_attention",
-        out_shape=jax.ShapeDtypeStruct(queries.shape, BF16),
+        out_shape=pltpu.VMEM(queries.shape, BF16),
         in_specs=[vmem_spec, vmem_spec, any_spec, any_spec],
-        out_specs=any_spec,
+        out_specs=vmem_spec,
         scratch_shapes=[
             pltpu.VMEM(queries.shape, BF16),
             pltpu.VMEM(key_value_rows.shape, BF16),
@@ -289,14 +320,13 @@
             pltpu.VMEM((Q_TILES, N_CTX, 16, HEAD_SIZE), BF16),
             pltpu.VMEM((2, 4, G, 4, UNITS, 16, HEAD_SIZE), BF16),
             pltpu.VMEM((QUERY_HEADS, UNITS, N_CTX, HEAD_SIZE), BF16),
-            pltpu.VMEM(queries.shape, BF16),
             pltpu.VMEM((2, N_CTX * 16, HEAD_SIZE), F32),
             pltpu.VMEM((SHARED, ROWS, HEAD_SIZE), F32),
             pltpu.VMEM((UNITS, N_CTX, 64 * G * UNITS), F32),
             pltpu.VMEM((UNITS, N_CTX, 64 * 4 * UNITS), F32),
-            pltpu.VMEM((UNITS, N_CTX, 64 * 4 * UNITS), F32),
+            pltpu.VMEM((UNITS, N_CTX, 64 * 2 * UNITS), F32),
+            pltpu.VMEM((UNITS, N_CTX, 64 * 2 * UNITS), F32),
             dma((2,)),
-            dma((KEY_VALUE_HEADS,)),
             dma((tiles,)),
             dma((tiles,)),
             dma((2, 4)),

time: 91.7 us -> 71.9 us (0.78)
  the two profiles are of different devices: /device:TPU:24 before, /device:TPU:1 now
where the time goes in v2:
time: 71.9 us; the launch traced here: 71.5 us
  Pallas kernels  70.4 us (98%)
  local copies, waits for them, and re-layouts  1.06 us (1%)
    pallas_call x1, Pallas kernels, local(): pl.pallas_call(kernel, name='repacked_attention', out_shape=pltpu.VMEM(qu...  70.4 us

profile of v2, /device:TPU:1, one launch (start us, length us, event | category | flops | bytes accessed | tf_op | source)
XLA Modules:
  0.0 71.5 jit_solution(7904566756319242456)
XLA Ops:
  0.0 70.4 %repacked_attention.1 = bf16[256,2560]{1,0:T(8,128)(2,1)S(1)} custom-call(s32[1,256]{1,0:T(1,128)} %bitcast.2, s32[1,256]{1,0:T(1,128)} %bitcast.3, bf16[256,2560]{1,0:T(8,128)(2,1)} %q_hbm.1, bf16[256,1024]{1,0:T(8,128)(2,1)} %kv_hbm.1), custom_call_target="tpu_custom_call" | custom-call | flops 5000000000 | bytes 4000000 | tf_op jit(solution)/shard_map/repacked_attention/pallas_call | solution.py:309
  70.4 1.1 %copy.6 = bf16[256,2560]{1,0:T(8,128)(2,1)} copy(bf16[256,2560]{1,0:T(8,128)(2,1)S(1)} %repacked_attention.1) | data formatting | bytes 2621440

commit v3 on v2

--- a/solution.py
+++ b/solution.py
@@ -22,7 +22,7 @@
 SLOT = {0: 0, 1: 1, 7: 2, 2: 3, 6: 4, 3: 5, 5: 6, 4: 7}
 REL = {slot: rel for rel, slot in SLOT.items()}
 Q_TILES = QUERY_HEADS // 4
-LEAD = 4
+LEAD = 5
 
 
 def z_offset(i):
@@ -33,7 +33,7 @@
 def kernel(
     slot_ref, doc_ref, q_hbm, kv_hbm, out_ref,
     q_in, kv_in, send, kv_got, q_got, gathered, q_heads,
-    stage, out_stage, bias_full, bias_a, bias_b, bias_c,
+    stage, out_stage, bias_a, bias_b, bias_c,
     in_sem, own_sem, send_sem, kv_sem, q_sem, ring_send, ring_recv,
 ):
     ctx, grp = lax.axis_index("ctx"), lax.axis_index("grp")
@@ -247,48 +247,45 @@
     prepare_q(1)
     pl.semaphore_wait(barrier, N_CTX - 1 + 2)
     issue(LEAD)
-    run([(0, 0, 0), (0, 1, 0), (0, 0, 1), (0, 2, 0), (0, 1, 1), (0, 3, 0), (0, 2, 1), (0, 0, 2), (0, 3, 1), (0, 1, 2)])
-    run([(1, 0, 0), (0, 2, 2), (0, 0, 3), (0, 3, 2), (0, 1, 3), (1, 1, 0), (1, 2, 0), (0, 2, 3), (0, 3, 3), (1, 3, 0)])
-    fill_bias(bias_full, 0, G)
+    state = {}
+
+    def stage_of(h, low, high, bias):
+        for k in range(UNITS):
+            state[h, k] = attend(h, k, low, high, bias, state.get((h, k)))
+            if high == G:
+                finish(h, k, state[h, k])
+
+    run([(0, 0, 0), (0, 1, 0), (0, 2, 0), (0, 0, 1), (0, 3, 0), (0, 1, 1), (1, 0, 0), (1, 1, 0), (0, 2, 1), (1, 2, 0)])
     fill_bias(bias_a, 0, 4)
+    run([(0, 3, 1), (1, 3, 0)])
     fill_bias(bias_b, 4, 6)
     fill_bias(bias_c, 6, G)
-    run([(1, 0, 1), (1, 1, 1)])
+    run([(1, 0, 1), (0, 0, 2), (1, 1, 1), (0, 1, 2), (1, 2, 1), (0, 2, 2)])
+    take_q(0)
+    run([(1, 3, 1), (0, 3, 2)])
+    take_q(1)
+    stage_of(0, 0, 4, bias_a)
+    run([(1, 0, 2), (0, 0, 3), (1, 1, 2), (0, 1, 3)])
+    take_q(2)
+    stage_of(1, 0, 4, bias_a)
+    run([(1, 2, 2), (0, 2, 3), (1, 3, 2), (0, 3, 3)])
+    stage_of(0, 4, 6, bias_b)
+    stage_of(1, 4, 6, bias_b)
+    run([(1, 0, 3), (1, 1, 3)])
+    issue(len(parts))
+    take_q(3)
+    stage_of(2, 0, 4, bias_a)
+    run([(1, 2, 3), (1, 3, 3)])
+    stage_of(2, 4, 6, bias_b)
     run([(0, p, 4) for p in range(4)])
-    take_q(0)
-    take_q(1)
-    finish(0, 0, attend(0, 0, 0, G, bias_full))
-    finish(0, 1, attend(0, 1, 0, G, bias_full))
-    run([(1, 2, 1)])
-    finish(0, 2, attend(0, 2, 0, G, bias_full))
-    run([(1, 3, 1)])
-    finish(0, 3, attend(0, 3, 0, G, bias_full))
-    run([(1, 0, 2), (1, 1, 2)])
-    issue(len(parts))
-    take_q(2)
-    finish(1, 0, attend(1, 0, 0, G, bias_full))
-    finish(1, 1, attend(1, 1, 0, G, bias_full))
-    run([(1, 2, 2)])
-    finish(1, 2, attend(1, 2, 0, G, bias_full))
-    run([(1, 3, 2)])
-    finish(1, 3, attend(1, 3, 0, G, bias_full))
-    run([(1, 0, 3), (1, 2, 3)])
-    take_q(3)
-    early = {}
-    for k in range(UNITS):
-        early[2, k] = attend(2, k, 0, 4, bias_a)
-    run([(1, 1, 3), (1, 3, 3)])
-    for k in range(UNITS):
-        early[2, k] = attend(2, k, 4, 6, bias_b, early[2, k])
+    stage_of(0, 6, G, bias_c)
+    stage_of(1, 6, G, bias_c)
     take_q(4)
-    for k in range(UNITS):
-        early[3, k] = attend(3, k, 0, 4, bias_a)
-    for k in range(UNITS):
-        early[3, k] = attend(3, k, 4, 6, bias_b, early[3, k])
+    stage_of(3, 0, 4, bias_a)
+    stage_of(3, 4, 6, bias_b)
     run([(1, p, 4) for p in range(4)])
-    for h in (2, 3):
-        for k in range(UNITS):
-            finish(h, k, attend(h, k, 6, G, bias_c, early[h, k]))
+    stage_of(2, 6, G, bias_c)
+    stage_of(3, 6, G, bias_c)
 
     for tile in range(2 + Q_TILES):
         piece = send.at[tile, pl.ds(0, N_CTX - 1)]
@@ -322,7 +319,6 @@
             pltpu.VMEM((QUERY_HEADS, UNITS, N_CTX, HEAD_SIZE), BF16),
             pltpu.VMEM((2, N_CTX * 16, HEAD_SIZE), F32),
             pltpu.VMEM((SHARED, ROWS, HEAD_SIZE), F32),
-            pltpu.VMEM((UNITS, N_CTX, 64 * G * UNITS), F32),
             pltpu.VMEM((UNITS, N_CTX, 64 * 4 * UNITS), F32),
             pltpu.VMEM((UNITS, N_CTX, 64 * 2 * UNITS), F32),
             pltpu.VMEM((UNITS, N_CTX, 64 * 2 * UNITS), F32),

time: 71.9 us -> 72.1 us (level)
  no operation moved by 1% of the time
where the time goes in v3:
time: 72.1 us; the launch traced here: 72 us
  Pallas kernels  70.9 us (98%)
  local copies, waits for them, and re-layouts  1.06 us (1%)
    pallas_call x1, Pallas kernels, local(): pl.pallas_call(kernel, name='repacked_attention', out_shape=pltpu.VMEM(qu...  70.9 us

profile of v3, /device:TPU:1, one launch (start us, length us, event | category | flops | bytes accessed | tf_op | source)
XLA Modules:
  0.0 72.0 jit_solution(12790643312032685851)
XLA Ops:
  0.0 70.9 %repacked_attention.1 = bf16[256,2560]{1,0:T(8,128)(2,1)S(1)} custom-call(s32[1,256]{1,0:T(1,128)} %bitcast.2, s32[1,256]{1,0:T(1,128)} %bitcast.3, bf16[256,2560]{1,0:T(8,128)(2,1)} %q_hbm.1, bf16[256,1024]{1,0:T(8,128)(2,1)} %kv_hbm.1), custom_call_target="tpu_custom_call" | custom-call | flops 5000000000 | bytes 4000000 | tf_op jit(solution)/shard_map/repacked_attention/pallas_call | solution.py:306
  70.9 1.1 %copy.6 = bf16[256,2560]{1,0:T(8,128)(2,1)} copy(bf16[256,2560]{1,0:T(8,128)(2,1)S(1)} %repacked_attention.1) | data formatting | bytes 2621440

commit v4 on v2

--- a/solution.py
+++ b/solution.py
@@ -47,7 +47,6 @@
     load_kv = pltpu.make_async_copy(kv_hbm, kv_in, in_sem.at[0])
     load_q = pltpu.make_async_copy(q_hbm, q_in, in_sem.at[1])
     load_kv.start()
-    load_q.start()
 
     barrier = pltpu.get_barrier_semaphore()
 
@@ -224,7 +223,7 @@
             if tile < 2:
                 send_kv(tile, p)
             else:
-                if p == 0 and tile >= 4:
+                if p == 0 and tile >= 3:
                     prepare_q(tile - 2)
                 send_q(tile - 2, p)
 
@@ -240,13 +239,14 @@
             issue(issued[0] + 1)
 
     load_kv.wait()
+    load_q.start()
     prepare_kv(0)
+    pl.semaphore_wait(barrier, N_CTX - 1 + 2)
+    issue(4)
     prepare_kv(1)
+    issue(LEAD)
     load_q.wait()
     prepare_q(0)
-    prepare_q(1)
-    pl.semaphore_wait(barrier, N_CTX - 1 + 2)
-    issue(LEAD)
     run([(0, 0, 0), (0, 1, 0), (0, 0, 1), (0, 2, 0), (0, 1, 1), (0, 3, 0), (0, 2, 1), (0, 0, 2), (0, 3, 1), (0, 1, 2)])
     run([(1, 0, 0), (0, 2, 2), (0, 0, 3), (0, 3, 2), (0, 1, 3), (1, 1, 0), (1, 2, 0), (0, 2, 3), (0, 3, 3), (1, 3, 0)])
     fill_bias(bias_full, 0, G)

time: 71.9 us -> 72.1 us (level)
  no operation moved by 1% of the time
where the time goes in v4:
time: 72.1 us; the launch traced here: 72 us
  Pallas kernels  70.9 us (98%)
  local copies, waits for them, and re-layouts  1.06 us (1%)
    pallas_call x1, Pallas kernels, local(): pl.pallas_call(kernel, name='repacked_attention', out_shape=pltpu.VMEM(qu...  70.9 us

profile of v4, /device:TPU:1, one launch (start us, length us, event | category | flops | bytes accessed | tf_op | source)
XLA Modules:
  0.0 72.0 jit_solution(14731281664665972027)
XLA Ops:
  0.0 70.9 %repacked_attention.1 = bf16[256,2560]{1,0:T(8,128)(2,1)S(1)} custom-call(s32[1,256]{1,0:T(1,128)} %bitcast.2, s32[1,256]{1,0:T(1,128)} %bitcast.3, bf16[256,2560]{1,0:T(8,128)(2,1)} %q_hbm.1, bf16[256,1024]{1,0:T(8,128)(2,1)} %kv_hbm.1), custom_call_target="tpu_custom_call" | custom-call | flops 5000000000 | bytes 4000000 | tf_op jit(solution)/shard_map/repacked_attention/pallas_call | solution.py:309
  70.9 1.1 %copy.6 = bf16[256,2560]{1,0:T(8,128)(2,1)} copy(bf16[256,2560]{1,0:T(8,128)(2,1)S(1)} %repacked_attention.1) | data formatting | bytes 2621440
